TPU v7x, 256 devices: a whole 4x4x8 slice. The times are simulated.
256 devices in a mesh: head: 8 (over y, x_lo), tok: 32 (over x_hi, z, core).
Axes of the slice: x: 4 (x_hi: 2, x_lo: 2; x = x_hi * 2 + x_lo), y: 4, z: 8, core: 2. Of those that a mesh axis runs over, the one named last changes fastest.
Arguments:
- head_outputs: bfloat16 [1024, 8192], P('tok', 'head'), may hold values from -6 to 6
- dec_bias: float32 [8192], P('head'), may hold values from -3 to 3
- enc_bias: float32 [65536], P('tok'), may hold values from -3 to 3
- enc_weight: bfloat16 [8192, 65536], P('head', 'tok'), may hold values from -0.0625 to 0.0625
- dec_weight: bfloat16 [65536, 8192], P('tok', 'head'), may hold values from -0.75 to 0.75
- out_weight: bfloat16 [8192, 8192], P('head', 'tok'), may hold values from -0.0625 to 0.0625
- active_ids: int32 [1024, 128], replicated, may hold values from 0 to 65535, as said below
Outputs:
- reconstruction: bfloat16 [1024, 8192], P('tok', 'head')
- projected: bfloat16 [1024, 8192], P('tok', 'head')
Inputs may be any that keep to these rules, and one draw needn't show every extreme that they name: `active_ids`: entry j of each row lies among the latents j * 512 to (j + 1) * 512 - 1, so the 128 entries of a row are different.
All inputs are finite; a program needn't handle non-finite values.
Results may differ from a plain program's by a relative error of at most 0.0061.
Values may be sent and summed in bfloat16 or wider, within the bound.
A program may use at most 128 MiB of HBM per device.

v0:
```python
import jax
import jax.numpy as jnp
from jax import lax
from jax.sharding import PartitionSpec as P


def latent_mask(id_rows, lat_start, lat_count):
    row_count = id_rows.shape[0]
    shifted = id_rows - lat_start
    inside = (shifted >= 0) & (shifted < lat_count)
    shifted = jnp.where(inside, shifted, lat_count)
    row_ids = jnp.arange(row_count, dtype=jnp.int32)[:, None]
    return jnp.zeros((row_count, lat_count), jnp.float32).at[row_ids, shifted].set(1.0, mode="drop")


def dense_decoder(latents, dec_weight):

    def decode(start, count):
        return jnp.dot(latents, dec_weight, preferred_element_type=jnp.float32)

    return decode


def on_device(head_outputs, dec_bias, enc_bias, enc_weight, dec_weight, out_weight, active_ids):
    centered = (head_outputs.astype(jnp.float32) - dec_bias[None, :]).astype(jnp.bfloat16)
    lat_count = enc_weight.shape[1]
    lat_start = lax.axis_index("tok") * lat_count
    partial_pre = jnp.dot(
        lax.all_gather(centered, "tok", axis=0, tiled=True),
        enc_weight,
        preferred_element_type=jnp.float32,
    )
    pre = lax.psum(partial_pre, "head") + enc_bias[None, :]
    mask = latent_mask(active_ids, lat_start, lat_count)
    latents = (mask * jnp.maximum(pre, 0.0)).astype(jnp.bfloat16)
    decode = dense_decoder(latents, dec_weight)
    decoded = lax.psum_scatter(
        decode(jnp.int32(0), head_outputs.shape[0] * lax.axis_size("tok")),
        "tok",
        scatter_dimension=0,
        tiled=True,
    )
    reconstruction = (decoded + dec_bias[None, :]).astype(jnp.bfloat16)
    partial_out = jnp.dot(
        reconstruction,
        lax.all_gather(out_weight, "tok", axis=1, tiled=True),
        preferred_element_type=jnp.float32,
    )
    projected = lax.psum_scatter(partial_out, "head", scatter_dimension=1, tiled=True).astype(
        jnp.bfloat16
    )
    return (reconstruction, projected)


def solution(mesh):
    return jax.shard_map(
        on_device,
        mesh=mesh,
        in_specs=(
            P("tok", "head"),
            P("head"),
            P("tok"),
            P("head", "tok"),
            P("tok", "head"),
            P("head", "tok"),
            P(),
        ),
        out_specs=(P("tok", "head"), P("tok", "head")),
        check_vma=False,
    )
```

profile of v0, /device:TPU:24, one launch (start us, length us, event | category | flops | bytes accessed | tf_op | source)
XLA Modules:
  0.0 945.3 jit_solution(17735549942467260121)
XLA Ops:
  7.2 0.0 all-gather.3.cloned.1.call-start
  7.2 1.5 subtract_convert_fusion
  8.7 0.0 all-gather.3.cloned.1.call-update
  8.7 0.0 all-reduce.2.cloned.1.call-start
  8.8 85.2 %all-gather.3.cloned.1.call-done = bf16[1024,1024]{1,0:T(8,128)(2,1)} async-done(((bf16[32,1024]{1,0:T(8,128)(2,1)}), bf16[1024,1024]{1,0:T(8,128)(2,1)}) %all-gather.3.cloned.1.call-update) | async-done | bytes 2097168 | tf_op jit(solution)/shard_map/all_gather | solution.py:29
  94.0 10.5 %fusion.7 = f32[1024,2048]{1,0:T(8,128)} fusion(bf16[1024,1024]{1,0:T(8,128)(2,1)} %all-gather.3.cloned.1.call-done, bf16[1024,2048]{1,0:T(8,128)(2,1)} %param.10), kind=kOutput, calls=%fused_computation.16 | convolution fusion | flops 4294967296 | bytes 14680064 | tf_op jit(solution)/shard_map/dot_general | solution.py:28
  104.5 0.0 copy-start
  104.5 0.0 copy-start.4
  104.6 0.0 copy-start.3
  104.6 0.0 all-reduce.2.cloned.1.call-update
  104.6 0.0 reduce-scatter.3.cloned.1.call-start
  104.6 1.0 copy-done
  105.6 0.1 fusion.5
  105.8 0.0 copy-done.4
  105.8 0.1 multiply_reduce_fusion
  105.9 0.0 copy-done.3
  105.9 0.3 and_reduce_fusion
  106.2 0.1 select_bitcast_fusion
  106.3 482.1 %scatter_custom_fusion = f32[2097152]{0:T(1024)} fusion(s32[131072]{0:T(1024)S(1)} %select_bitcast_fusion, f32[131072]{0:T(1024)S(1)} %broadcast.26, f32[]{:T(128)} %constant.5.clone.1), kind=kCustom, calls=%fused_computation.3 | custom fusion | bytes 8388612
  588.4 0.0 copy-start.5
  588.4 9.3 reshape.11
  597.7 0.0 copy-start.2
  597.7 0.0 all-reduce.2.cloned.1.call-done
  597.7 0.0 copy-done.5
  597.7 13.4 %fusion = f32[1024,1024]{1,0:T(8,128)} fusion(bf16[2048,1024]{1,0:T(8,128)(2,1)} %param.11, f32[1024,2048]{1,0:T(8,128)} %reshape.11, f32[1024,2048]{1,0:T(8,128)} %all-reduce.2.cloned.1.call-done, f32[2048]{0:T(1024)S(1)} %copy-done.5), kind=kOutput, calls=%fused_computation.2 | convolution fusion | flops 4303355904 | bytes 25174016 | tf_op jit(solution)/shard_map/dot_general | solution.py:19
  611.1 0.0 reduce-scatter.3.cloned.1.call-update
  611.1 0.0 all-gather.5.cloned.1.call-start
  611.1 0.5 all-gather.5.cloned.1.call-update
  611.7 0.2 reduce-scatter.5.cloned.1.call-start
  611.9 124.0 %reduce-scatter.3.cloned.1.call-done = f32[32,1024]{1,0:T(8,128)} async-done(((f32[1024,1024]{1,0:T(8,128)}), f32[32,1024]{1,0:T(8,128)}) %reduce-scatter.3.cloned.1.call-update) | async-done | bytes 131088 | tf_op jit(solution)/shard_map/reduce_scatter | solution.py:37
  735.9 0.0 copy-done.2
  735.9 0.9 add_convert_fusion
  736.8 0.0 copy-start.1
  736.8 152.3 %all-gather.5.cloned.1.call-done = bf16[1024,8192]{1,0:T(8,128)(2,1)} async-done(((bf16[1024,256]{1,0:T(8,128)(2,1)}), bf16[1024,8192]{1,0:T(8,128)(2,1)}) %all-gather.5.cloned.1.call-update) | async-done | bytes 16777232 | tf_op jit(solution)/shard_map/all_gather | solution.py:46
  889.2 9.7 %fusion.8 = f32[32,8192]{1,0:T(8,128)} fusion(bf16[32,1024]{1,0:T(8,128)(2,1)S(1)} %add_convert_fusion, bf16[1024,8192]{1,0:T(8,128)(2,1)} %all-gather.5.cloned.1.call-done), kind=kOutput, calls=%fused_computation.17 | convolution fusion | flops 536870912 | bytes 17891328 | tf_op jit(solution)/shard_map/dot_general | solution.py:44
  898.9 0.0 copy-done.1
  898.9 0.0 reduce-scatter.5.cloned.1.call-update
  898.9 38.3 %reduce-scatter.5.cloned.1.call-done = f32[32,1024]{1,0:T(8,128)} async-done(((f32[32,8192]{1,0:T(8,128)}), f32[32,1024]{1,0:T(8,128)}) %reduce-scatter.5.cloned.1.call-update) | async-done | bytes 131088 | tf_op jit(solution)/shard_map/reduce_scatter | solution.py:49
  937.2 1.5 convert_element_type.19
  (2 shorter events, 0.1 us)
Async XLA Ops:
  7.2 86.8 %all-gather.3.cloned.1.call-start = ((), (), s32[]{:S(2)}) async-start(), calls=%async_computation.2 | async-start | bytes 2162688 | tf_op jit(solution)/shard_map/all_gather | solution.py:29
  8.7 589.0 %all-reduce.2.cloned.1.call-start = ((), (), s32[]{:S(2)}) async-start(), calls=%async_computation.3 | async-start | bytes 16777216 | tf_op jit(solution)/shard_map/psum | solution.py:33
  104.5 1.0 copy-start
  104.5 1.2 copy-start.4
  104.6 1.4 copy-start.3
  104.6 631.3 %reduce-scatter.3.cloned.1.call-start = ((), (), s32[]{:S(2)}) async-start(), calls=%async_computation.4 | async-start | bytes 4325376 | tf_op jit(solution)/shard_map/reduce_scatter | solution.py:37
  588.4 9.3 copy-start.5
  597.7 138.2 %copy-start.2 = (f32[1024]{0:T(1024)S(1)}, f32[1024]{0:T(1024)}, u32[]{:S(2)}) copy-start(f32[1024]{0:T(1024)} %param.8) | copy-start | bytes 12292
  611.1 278.1 %all-gather.5.cloned.1.call-start = ((), (), s32[]{:S(2)}) async-start(), calls=%async_computation.5 | async-start | bytes 17301504 | tf_op jit(solution)/shard_map/all_gather | solution.py:46
  611.7 325.6 %reduce-scatter.5.cloned.1.call-start = ((), (), s32[]{:S(2)}) async-start(), calls=%async_computation.6 | async-start | bytes 1179648 | tf_op jit(solution)/shard_map/reduce_scatter | solution.py:49
  736.8 162.1 %copy-start.1 = (bf16[32,1024]{1,0:T(8,128)(2,1)}, bf16[32,1024]{1,0:T(8,128)(2,1)S(1)}, u32[]{:S(2)}) copy-start(bf16[32,1024]{1,0:T(8,128)(2,1)S(1)} %add_convert_fusion) | copy-start | bytes 196612
Sparse Core Ops, SparseCore 0:
  11.3 82.6 all-gather.2
  104.7 341.1 all-reduce.1
  611.2 124.6 reduce-scatter.2
  738.6 150.4 all-gather.4
  899.0 38.1 reduce-scatter.4
where the time goes:
time: 948 us; the launch traced here: 945 us
  local copies, waits for them, and re-layouts  492 us (52%)
  waiting for transfers between devices  400 us (42%)
  matrix products  33.7 us (4%)
  between operations  13.8 us (1%)
    unnamed x14, local copies, waits for them, and re-layouts  483 us
    all_gather x1, waiting for transfers between devices, on_device(): lax.all_gather(out_weight, 'tok', axis=1, tiled=True)  152 us
    reduce_scatter x1, waiting for transfers between devices, on_device(): lax.psum_scatter(decode(jnp.int32(0), head_outputs.shape[0] * lax.axis_si...  124 us
    all_gather x1, waiting for transfers between devices, on_device(): lax.all_gather(centered, 'tok', axis=0, tiled=True)  85.2 us
    reduce_scatter x1, waiting for transfers between devices, on_device(): lax.psum_scatter(partial_out, 'head', scatter_dimension=1, tiled=True)  38.3 us
  transfers between devices with their start and end apart: 5, of which 4 were waited for; matrix products, arithmetic and copies ran while one was open for 52% of the time, Pallas kernels for 0%

commit v1 on v0

v1 whole, which is shorter than its diff:
```python
import jax
import jax.numpy as jnp
from jax import lax
from jax.sharding import PartitionSpec as P


def on_device(head_outputs, dec_bias, enc_bias, enc_weight, dec_weight, out_weight, active_ids):
    tokens, per_token = active_ids.shape
    lat_count = enc_weight.shape[1]
    stride = lat_count * lax.axis_size("tok") // per_token
    here = lat_count // stride
    tok = lax.axis_index("tok")

    centered = (head_outputs.astype(jnp.float32) - dec_bias[None, :]).astype(jnp.bfloat16)
    partial_pre = jnp.dot(
        lax.all_gather(centered, "tok", axis=0, tiled=True),
        enc_weight,
        preferred_element_type=jnp.float32,
    ).reshape(tokens, here, stride)
    ids = lax.dynamic_slice(active_ids, (0, tok * here), (tokens, here))
    offset = ids - (tok * here + jnp.arange(here, dtype=jnp.int32))[None, :] * stride
    active = offset[:, :, None] == jnp.arange(stride, dtype=jnp.int32)[None, None, :]
    picked = jnp.sum(jnp.where(active, partial_pre, 0.0), axis=2)
    bias = jnp.sum(jnp.where(active, enc_bias.reshape(1, here, stride), 0.0), axis=2)
    value = jnp.maximum(lax.psum(picked, "head") + bias, 0.0)
    latents = jnp.where(active, value[:, :, None], 0.0).astype(jnp.bfloat16)
    decoded = lax.psum_scatter(
        jnp.dot(latents.reshape(tokens, lat_count), dec_weight, preferred_element_type=jnp.float32),
        "tok",
        scatter_dimension=0,
        tiled=True,
    )
    reconstruction = (decoded + dec_bias[None, :]).astype(jnp.bfloat16)
    partial_out = jnp.dot(
        lax.all_gather(reconstruction, "tok", axis=0, tiled=True),
        out_weight,
        preferred_element_type=jnp.float32,
    )
    mine = lax.all_to_all(partial_out, "tok", split_axis=0, concat_axis=1, tiled=True)
    projected = lax.psum_scatter(mine, "head", scatter_dimension=1, tiled=True).astype(jnp.bfloat16)
    return (reconstruction, projected)


def solution(mesh):
    return jax.shard_map(
        on_device,
        mesh=mesh,
        in_specs=(
            P("tok", "head"),
            P("head"),
            P("tok"),
            P("head", "tok"),
            P("tok", "head"),
            P("head", "tok"),
            P(),
        ),
        out_specs=(P("tok", "head"), P("tok", "head")),
        check_vma=False,
    )
```

time: 948 us -> 481 us (0.51)
  local copies, waits for them, and re-layouts: 492 us -> 24.9 us
  waiting for transfers between devices: 400 us -> 318 us
  blocking collectives: 0 us -> 75.7 us
  other arithmetic: 4.53 us -> 23.1 us
  matrix products: 33.7 us -> 22.5 us
    unnamed x14 -> x10, local copies, waits for them, and re-layouts: 483 us -> 9.52 us
    all_gather x1, waiting for transfers between devices: 152 us -> 80 us  [on_device(): lax.all_gather(reconstruction, 'tok', axis=0, tiled=True)]
    psum x0 -> x1, blocking collectives: none -> 41.5 us  [on_device(): value = jnp.maximum(lax.psum(picked, 'head') + bias, 0.0)]
    all_to_all x0 -> x1, blocking collectives: none -> 34.2 us  [on_device(): lax.all_to_all(partial_out, 'tok', split_axis=0, concat_axis=1, tiled=True)]
    reduce_sum x0 -> x1, other arithmetic: none -> 17.2 us  [on_device(): jnp.sum(jnp.where(active, enc_bias.reshape(1, here, stride), 0.0), axis=2)]
    dot_general x2, matrix products: 23.1 us -> 12 us  [the longest x1 9.66 us: on_device(): jnp.dot(latents.reshape(tokens, lat_count), dec_weight, preferred_element...]
    reshape x0 -> x1, local copies, waits for them, and re-layouts: none -> 10.8 us  [on_device(): partial_pre = jnp.dot(lax.all_gather(centered, 'tok', axis=0, tiled=True)...]
    all_gather x1, waiting for transfers between devices: 85.2 us -> 74.5 us  [on_device(): lax.all_gather(centered, 'tok', axis=0, tiled=True)]
  transfers between devices with their start and end apart: 5 -> 4, of which waited for: 4 -> 4; matrix products, arithmetic and copies ran while one was open for 52% -> 2% of each run, Pallas kernels for 0% -> 0%
where the time goes in v1:
time: 481 us; the launch traced here: 478 us
  waiting for transfers between devices  318 us (66%)
  blocking collectives  75.7 us (16%)
  local copies, waits for them, and re-layouts  24.9 us (5%)
  other arithmetic  23.1 us (5%)
  matrix products  22.5 us (5%)
  between operations  13.8 us (3%)
    reduce_scatter x1, waiting for transfers between devices, on_device(): lax.psum_scatter(jnp.dot(latents.reshape(tokens, lat_count), dec_weight,...  125 us
    all_gather x1, waiting for transfers between devices, on_device(): lax.all_gather(reconstruction, 'tok', axis=0, tiled=True)  80 us
    all_gather x1, waiting for transfers between devices, on_device(): lax.all_gather(centered, 'tok', axis=0, tiled=True)  74.5 us
    psum x1, blocking collectives, on_device(): value = jnp.maximum(lax.psum(picked, 'head') + bias, 0.0)  41.5 us
    reduce_scatter x1, waiting for transfers between devices, on_device(): lax.psum_scatter(mine, 'head', scatter_dimension=1, tiled=True)  38.3 us
    all_to_all x1, blocking collectives, on_device(): lax.all_to_all(partial_out, 'tok', split_axis=0, concat_axis=1, tiled=True)  34.2 us
    reduce_sum x1, other arithmetic, on_device(): jnp.sum(jnp.where(active, enc_bias.reshape(1, here, stride), 0.0), axis=2)  17.2 us
    reshape x1, local copies, waits for them, and re-layouts, on_device(): partial_pre = jnp.dot(lax.all_gather(centered, 'tok', axis=0, tiled=True)...  10.8 us
  transfers between devices with their start and end apart: 4, of which 4 were waited for; matrix products, arithmetic and copies ran while one was open for 2% of the time, Pallas kernels for 0%

profile of v1, /device:TPU:24, one launch (start us, length us, event | category | flops | bytes accessed | tf_op | source)
XLA Modules:
  0.0 478.3 jit_solution(10567050378219615440)
XLA Ops:
  7.2 0.0 copy-start
  7.2 0.0 all-gather.3.cloned.1.call-start
  7.2 1.5 subtract_convert_fusion
  8.8 0.0 all-gather.3.cloned.1.call-update
  8.8 0.0 reduce-scatter.3.cloned.1.call-start
  8.8 0.7 broadcast_in_dim.37
  9.6 1.2 dynamic-slice_subtract_fusion
  10.8 1.4 eq.24
  12.2 7.3 %copy.11 = s32[128,8,4,512]{3,1,2,0:T(8,128)} copy(s32[128,8,4,512]{3,2,1,0:T(4,128)S(1)} %bitcast.16) | data formatting | bytes 16777216
  19.5 74.5 %all-gather.3.cloned.1.call-done = bf16[1024,1024]{1,0:T(8,128)(2,1)} async-done(((bf16[32,1024]{1,0:T(8,128)(2,1)}), bf16[1024,1024]{1,0:T(8,128)(2,1)}) %all-gather.3.cloned.1.call-update) | async-done | bytes 2097168 | tf_op jit(solution)/shard_map/all_gather | solution.py:16
  94.0 10.5 %fusion.4 = f32[1024,2048]{1,0:T(8,128)} fusion(bf16[1024,1024]{1,0:T(8,128)(2,1)} %all-gather.3.cloned.1.call-done, bf16[1024,2048]{1,0:T(8,128)(2,1)} %param.10), kind=kOutput, calls=%fused_computation.14 | convolution fusion | flops 4294967296 | bytes 14680064 | tf_op jit(solution)/shard_map/dot_general | solution.py:15
  104.6 10.8 %reshape.25 = f32[1024,4,512]{2,1,0:T(4,128)} reshape(f32[1024,2048]{1,0:T(8,128)} %fusion.4) | data formatting | bytes 16777216 | tf_op jit(solution)/shard_map/reshape | solution.py:19
  115.4 17.2 %select_reduce_fusion = (f32[1024,4]{1,0:T(8,128)S(1)}, f32[1024,4]{1,0:T(8,128)S(1)}) fusion(f32[4,512]{1,0:T(4,128)S(1)} %broadcast_in_dim.37, s32[1024,4]{1,0:T(8,128)S(1)} %dynamic-slice_subtract_fusion, f32[1024,4,512]{2,1,0:T(4,128)} %reshape.25), kind=kLoop, calls=%fused_computation.1 | loop fusion | flops 10477568 | bytes 8445952 | tf_op jit(solution)/shard_map/reduce_sum | solution.py:24
  132.5 41.5 %psum.7 = f32[1024,4]{1,0:T(8,128)S(1)} all-reduce(f32[1024,4]{1,0:T(8,128)S(1)} %get-tuple-element.3), channel_id=1, replica_groups=mesh['head'=8,'tok'=32] {'head'}, use_global_device_ids=true, to_apply=%region_1.2 | all-reduce | flops 4096 | bytes 32768 | tf_op jit(solution)/shard_map/psum | solution.py:25
  174.0 0.1 add_maximum_fusion
  174.1 1.4 broadcast_in_dim.39
  175.5 0.0 copy-start.2
  175.5 1.4 copy.13
  177.0 0.7 copy-done.2
  177.7 9.7 %fusion = f32[1024,1024]{1,0:T(8,128)} fusion(bf16[2048,1024]{1,0:T(8,128)(2,1)S(1)} %copy-done.2, bf16[1024,2048]{1,0:T(8,128)(2,1)S(1)} %bitcast.19, s32[1024,2048]{1,0:T(8,128)} %bitcast.18, s32[2048]{0:T(1024)S(1)} %bitcast.23), kind=kOutput, calls=%fused_computation.4 | convolution fusion | flops 4299161600 | bytes 20979712 | tf_op jit(solution)/shard_map/dot_general | solution.py:28
  187.4 0.0 copy-start.1
  187.4 0.0 reduce-scatter.3.cloned.1.call-update
  187.4 0.0 all-gather.5.cloned.1.call-start
  187.4 125.2 %reduce-scatter.3.cloned.1.call-done = f32[32,1024]{1,0:T(8,128)} async-done(((f32[1024,1024]{1,0:T(8,128)}), f32[32,1024]{1,0:T(8,128)}) %reduce-scatter.3.cloned.1.call-update) | async-done | bytes 131088 | tf_op jit(solution)/shard_map/reduce_scatter | solution.py:27
  312.6 0.0 copy-done.1
  312.6 1.5 add_convert_fusion
  314.1 0.0 all-gather.5.cloned.1.call-update
  314.2 0.0 reduce-scatter.5.cloned.1.call-start
  314.2 80.0 %all-gather.5.cloned.1.call-done = bf16[1024,1024]{1,0:T(8,128)(2,1)} async-done(((bf16[32,1024]{1,0:T(8,128)(2,1)}), bf16[1024,1024]{1,0:T(8,128)(2,1)}) %all-gather.5.cloned.1.call-update) | async-done | bytes 2097168 | tf_op jit(solution)/shard_map/all_gather | solution.py:35
  394.2 0.0 copy-done
  394.2 2.3 fusion.5
  396.5 34.2 %all_to_all.19 = f32[32,32,256]{2,1,0:T(8,128)S(1)} all-to-all(f32[32,32,256]{2,1,0:T(8,128)S(1)} %bitcast.22), channel_id=1, replica_groups=mesh['head'=8,'tok'=32] {'tok'}, dimensions={0} | all-to-all | bytes 2097152 | tf_op jit(solution)/shard_map/all_to_all | solution.py:39
  430.8 1.1 copy.10
  431.8 0.0 reduce-scatter.5.cloned.1.call-update
  431.9 38.3 %reduce-scatter.5.cloned.1.call-done = f32[32,1024]{1,0:T(8,128)} async-done(((f32[32,8192]{1,0:T(8,128)}), f32[32,1024]{1,0:T(8,128)}) %reduce-scatter.5.cloned.1.call-update) | async-done | bytes 131088 | tf_op jit(solution)/shard_map/reduce_scatter | solution.py:40
  470.2 1.5 convert_element_type.20
  (3 shorter events, 0.0 us)
Async XLA Ops:
  7.2 387.1 %copy-start = (bf16[1024,256]{1,0:T(8,128)(2,1)S(1)}, bf16[1024,256]{1,0:T(8,128)(2,1)}, u32[]{:S(2)}) copy-start(bf16[1024,256]{1,0:T(8,128)(2,1)} %param.12) | copy-start | bytes 1572868
  7.2 86.8 %all-gather.3.cloned.1.call-start = ((), (), s32[]{:S(2)}) async-start(), calls=%async_computation.3 | async-start | bytes 2162688 | tf_op jit(solution)/shard_map/all_gather | solution.py:16
  8.8 303.8 %reduce-scatter.3.cloned.1.call-start = ((), (), s32[]{:S(2)}) async-start(), calls=%async_computation.4 | async-start | bytes 4325376 | tf_op jit(solution)/shard_map/reduce_scatter | solution.py:27
  175.5 2.2 copy-start.2
  187.4 125.2 %copy-start.1 = (f32[1024]{0:T(1024)S(1)}, f32[1024]{0:T(1024)}, u32[]{:S(2)}) copy-start(f32[1024]{0:T(1024)} %param.8) | copy-start | bytes 12292
  187.4 206.8 %all-gather.5.cloned.1.call-start = ((), (), s32[]{:S(2)}) async-start(), calls=%async_computation.5 | async-start | bytes 2162688 | tf_op jit(solution)/shard_map/all_gather | solution.py:35
  314.2 156.1 %reduce-scatter.5.cloned.1.call-start = ((), (), s32[]{:S(2)}) async-start(), calls=%async_computation.6 | async-start | bytes 1179648 | tf_op jit(solution)/shard_map/reduce_scatter | solution.py:40
Sparse Core Ops, SparseCore 0:
  11.4 82.6 all-gather.2
  187.5 125.0 reduce-scatter.2
  316.3 77.8 all-gather.4
  432.0 38.1 reduce-scatter.4

commit v2 on v1

v2 whole, which is shorter than its diff:
```python
import jax
import jax.numpy as jnp
from jax import lax
from jax.experimental import pallas as pl
from jax.experimental.pallas import tpu as pltpu
from jax.sharding import PartitionSpec as P

MESH = pl.DeviceIdType.MESH
F32, BF16 = jnp.float32, jnp.bfloat16

HEADS = 8
TOKENS, WIDTH, BLOCK = 1024, 1024, 32
LATS, HERE, STRIDE = 2048, 4, 512
COLS = 256
PLANE = 128
PLANES = (0, -1, 1, -2, 2, -3, 3, 4)
GROUPS = ((0, 1), (1, 2), (3, 2), (5, 2), (7, 1))
MESSAGES = 192


def row_of(slot, core, side):
    return PLANE * slot + 64 * core + BLOCK * side


def kernel(
    ho, dbias, ebias, ew, dw, ow, ids,
    rec_out, proj_out,
    ho_v, db_v, eb_v, ew_v, dw_v, ow_v, ids_v,
    cen, off, vals, packed, lat, own_part, core_out, core_in,
    zp_out, zp_in, zm_out, zm_in, x_out, x_in, rec,
    part, part_in, piece, piece_in, proj_v,
    load_sem, send_sem, recv_sem, last_recv, store_sem,
):
    h = lax.axis_index("head")
    t = lax.axis_index("tok")
    core, z, side = t % 2, (t // 2) % 8, t // 16

    def tok_of(dside, dz, dcore):
        return ((side + dside) % 2) * 16 + ((z + dz) % 8) * 2 + (core + dcore) % 2

    zp, zm = {"tok": tok_of(0, 1, 0)}, {"tok": tok_of(0, 7, 0)}
    xn, cn = {"tok": tok_of(1, 0, 0)}, {"tok": tok_of(0, 0, 1)}
    heads = [(h + k) % HEADS for k in range(HEADS)]
    out_head = t // 4
    my_part = h // 2
    final_tok = [tok_of(my_part % 2, PLANES[s] % 8, my_part // 2) for s in range(8)]
    to_self = (out_head == h) & (my_part == 0)

    loads = []
    for n, (src, dst) in enumerate(
        ((ho, ho_v), (dbias, db_v), (ids, ids_v), (ebias, eb_v), (ew, ew_v), (dw, dw_v), (ow, ow_v))
    ):
        loads.append(pltpu.make_async_copy(src, dst, load_sem.at[n]))
        loads[-1].start()

    barrier = pltpu.get_barrier_semaphore()
    for target in (zp, zm, xn, cn):
        pl.semaphore_signal(barrier, inc=1, device_id=target, device_id_type=MESH)
    for k in range(1, HEADS):
        pl.semaphore_signal(barrier, inc=1, device_id={"head": heads[k]}, device_id_type=MESH)
    for s in range(8):
        target = {"head": out_head, "tok": final_tok[s]}
        pl.semaphore_signal(barrier, inc=1, device_id=target, device_id_type=MESH)

    loads[0].wait()
    loads[1].wait()
    cen[pl.ds(0, BLOCK), :] = (ho_v[...].astype(F32) - db_v[...]).astype(BF16)
    vals[...] = jnp.zeros_like(vals)
    pl.semaphore_wait(barrier, 4 + 7 + 8)

    sent = []

    def send(src, dst, target):
        n = len(sent)
        copy = pltpu.make_async_remote_copy(
            src_ref=src, dst_ref=dst, send_sem=send_sem.at[n], recv_sem=recv_sem.at[n],
            device_id=target, device_id_type=MESH,
        )
        copy.start()
        sent.append(copy)
        return copy

    def gather(buf, crossed):
        def block(slot, core, side):
            return buf.at[pl.ds(row_of(slot, core, side), BLOCK), :]

        def cross(slot, side):
            crossed[slot, side] = send(block(slot, 0, side), block(slot, 1, side), cn)

        plus, minus = {}, {}

        def go_plus(k, side):
            if k == 3 and side == 1:
                return
            plus[k, side] = send(
                block(2 * k - 1 if k else 0, 0, side), block(2 * k + 1, 0, side), zp
            )

        def go_minus(k, side):
            if k == 3 and side == 0:
                return
            minus[k, side] = send(
                block(2 * k, 0, side), block(2 * k + 2 if k < 3 else 7, 0, side), zm
            )

        over = send(block(0, 0, 0), block(0, 0, 1), xn)
        go_plus(0, 0)
        go_minus(0, 0)
        cross(0, 0)
        yield
        over.wait_recv()
        go_plus(0, 1)
        go_minus(0, 1)
        cross(0, 1)
        yield
        for k in range(1, 4):
            for side in range(2):
                plus[k - 1, side].wait_recv()
                go_plus(k, side)
                cross(2 * k - 1, side)
                minus[k - 1, side].wait_recv()
                go_minus(k, side)
                cross(2 * k, side)
                yield
        plus[3, 0].wait_recv()
        cross(7, 0)
        minus[3, 1].wait_recv()
        cross(7, 1)
        yield

    def whole(crossed, slots):
        for slot in slots:
            for side in range(2):
                crossed[slot, side].wait_recv()

    lane = lax.broadcasted_iota(jnp.int32, (PLANE, 128), 1)
    lane_f = lane.astype(F32)

    crossed = {}
    steps = gather(cen, crossed)
    next(steps)
    loads[2].wait()

    def offsets(slot):
        row = lambda q: pl.multiple_of(
            ((side + q % 2) % 2) * 512 + ((z + PLANES[slot] % 8) % 8) * 64 + ((core + q // 2) % 2) * BLOCK,
            BLOCK,
        )
        here = jnp.concatenate([ids_v[pl.ds(row(q), BLOCK), :] for q in range(4)], axis=0)
        here = (here - t * LATS).astype(F32)
        for j in range(HERE):
            column = jnp.sum(jnp.where(lane == t * HERE + j, here, 0.0), axis=1, keepdims=True)
            off[j, pl.ds(PLANE * slot, PLANE), :] = jnp.broadcast_to(column - j * STRIDE, (PLANE, 128))

    for slot in range(4):
        offsets(slot)
    next(steps)
    for slot in range(4, 8):
        offsets(slot)
    loads[3].wait()
    eb_v[...] = eb_v[...] * jnp.where(h == 0, 1.0, 0.0)

    def encode(group, first, last):
        slot, count = group
        rows = pl.ds(PLANE * slot, PLANE * count)
        lane_g = lax.broadcasted_iota(jnp.int32, (PLANE * count, 128), 1)
        lane_gf = lane_g.astype(F32)

        def body(j, carry):
            lats = pl.ds(pl.multiple_of(j * STRIDE, STRIDE), STRIDE)
            pre = jnp.dot(cen[rows, :], ew_v[:, lats], preferred_element_type=F32) + eb_v[:, lats]
            where = off[j, rows, :]
            total = jnp.zeros((PLANE * count, 128), F32)
            for q in range(4):
                total += jnp.where(lane_gf + 128.0 * q == where, pre[:, 128 * q:128 * (q + 1)], 0.0)
            picked = jnp.sum(total, axis=1, keepdims=True)
            vals[rows, :] += jnp.where(lane_g == j, picked, 0.0)
            return carry

        lax.fori_loop(first, last, body, 0)

    def pack(slot):
        packed[0, :, pl.ds(PLANE * slot, PLANE)] = vals[pl.ds(PLANE * slot, PLANE), :].T[:8, :]

    def pack(slots):
        for slot in slots:
            rows = pl.ds(PLANE * slot, PLANE)
            packed[0, :, rows] = vals[rows, :].T[:8, :]
        lanes = pl.ds(PLANE * slots[0], PLANE * len(slots))
        for k in range(1, HEADS):
            arrived[slots[0], k] = send(
                packed.at[0, :, lanes], packed.at[k, :, lanes], {"head": heads[k]}
            )

    arrived = {}
    loads[4].wait()
    for n in range(3):
        slot, count = GROUPS[n]
        next(steps)
        whole(crossed, range(slot, slot + count))
        encode(GROUPS[n], 0, 2)
        next(steps)
        encode(GROUPS[n], 2, 4)
    next(steps)
    pack(range(0, 5))
    whole(crossed, (5, 6))
    encode(GROUPS[3], 0, 4)
    pack((5, 6))
    whole(crossed, (7,))
    encode(GROUPS[4], 0, 4)
    pack((7,))

    loads[5].wait()
    crossed_sums = {}

    def decode(group):
        slot, count = group

        def fill(i, carry):
            rows = pl.ds(pl.multiple_of(PLANE * (slot + i), PLANE), PLANE)
            total = packed[0, :, rows]
            for k in range(1, HEADS):
                total += packed[k, :, rows]
            value = jnp.concatenate(
                [jnp.maximum(total, 0.0), jnp.zeros((PLANE - 8, PLANE), F32)], axis=0
            ).T
            for j in range(HERE):
                column = jnp.broadcast_to(value[:, j:j + 1], (PLANE, 128))
                where = off[j, rows, :]
                for q in range(4):
                    lat[pl.ds(pl.multiple_of(PLANE * i, PLANE), PLANE),
                        STRIDE * j + 128 * q:STRIDE * j + 128 * (q + 1)] = jnp.where(
                            lane_f + 128.0 * q == where, column, 0.0).astype(BF16)
            return carry

        lax.fori_loop(0, count, fill, 0)

        def body(n, carry):
            cols = pl.ds(pl.multiple_of(n * 256, 256), 256)
            total = jnp.dot(lat[pl.ds(0, PLANE * count), :], dw_v[:, cols], preferred_element_type=F32)
            for i in range(count):
                own_part[slot + i, :, cols] = total[PLANE * i:PLANE * i + 64]
                core_out[slot + i, :, cols] = total[PLANE * i + 64:PLANE * (i + 1)].astype(BF16)
            return carry

        lax.fori_loop(0, WIDTH // 256, body, 0)
        for i in range(count):
            crossed_sums[slot + i] = send(core_out.at[slot + i], core_in.at[slot + i], cn)

    def summed(slot, side):
        rows = pl.ds(BLOCK * side, BLOCK)
        return own_part[slot, rows, :] + core_in[slot, rows, :].astype(F32)

    plus, minus = {}, {}

    def ring(out, arrived_at, table, target, n, slot, side, before):
        total = summed(slot, side)
        if before is not None:
            table[before].wait_recv()
            total += arrived_at[before].astype(F32)
        out[n] = total.astype(BF16)
        table[n] = send(out.at[n], arrived_at.at[n], target)

    def go_plus(n, slot, side, before):
        ring(zp_out, zp_in, plus, zp, n, slot, side, before)

    def go_minus(n, slot, side, before):
        ring(zm_out, zm_in, minus, zm, n, slot, side, before)

    def get(slot):
        for k in range(1, HEADS):
            arrived[slot, k].wait_recv()

    get(7)
    decode((7, 1))
    get(5)
    crossed_sums[7].wait_recv()
    go_plus(0, 7, 1, None)
    go_minus(0, 7, 0, None)
    decode((5, 2))
    get(0)
    crossed_sums[5].wait_recv()
    crossed_sums[6].wait_recv()
    go_plus(2, 6, 0, None)
    go_minus(1, 5, 1, None)
    go_plus(1, 6, 1, 0)
    go_minus(2, 5, 0, 0)
    decode((3, 2))
    crossed_sums[3].wait_recv()
    crossed_sums[4].wait_recv()
    go_minus(3, 3, 1, 1)
    go_plus(4, 4, 0, 2)
    go_plus(3, 4, 1, 1)
    go_minus(4, 3, 0, 2)
    decode((1, 2))
    crossed_sums[1].wait_recv()
    crossed_sums[2].wait_recv()
    go_minus(5, 1, 1, 3)
    go_plus(5, 2, 1, 3)
    go_plus(6, 2, 0, 4)
    go_minus(6, 1, 0, 4)
    decode((0, 1))
    crossed_sums[0].wait_recv()

    def own(side, n):
        plus[n].wait_recv()
        minus[n].wait_recv()
        return summed(0, side) + (zp_in[n].astype(F32) + zm_in[n].astype(F32))

    x_out[...] = own(1, 5).astype(BF16)
    x_sum = send(x_out, x_in, xn)
    mine = own(0, 6) + db_v[...]
    x_sum.wait_recv()
    rec[pl.ds(0, BLOCK), :] = (mine + x_in[...].astype(F32)).astype(BF16)

    crossed = {}
    steps = gather(rec, crossed)
    next(steps)
    store_rec = pltpu.make_async_copy(rec.at[pl.ds(0, BLOCK), :], rec_out, store_sem.at[0])
    store_rec.start()
    loads[6].wait()
    spread = {}

    def project(group):
        slot, count = group
        out = jnp.dot(
            rec[pl.ds(PLANE * slot, PLANE * count), :], ow_v[...], preferred_element_type=F32
        ).astype(BF16)
        for i in range(count):
            part[slot + i] = out[PLANE * i:PLANE * (i + 1)]
        for k in range(1, HEADS):
            rows = pl.ds(pl.multiple_of(heads[k] * 16, 16), 16)
            spread[slot, k] = send(
                part.at[pl.ds(slot, count), rows, :],
                part_in.at[k, pl.ds(slot, count)],
                {"head": heads[k]},
            )

    def finish(group):
        slot, count = group
        for k in range(1, HEADS):
            spread[slot, k].wait_recv()
        rows = pl.ds(pl.multiple_of(h * 16, 16), 16)
        for s in range(slot, slot + count):
            total = part[s, rows, :].astype(F32)
            for k in range(1, HEADS):
                total += part_in[k, s].astype(F32)
            piece[s] = total.astype(BF16)
            n = len(sent)
            sent.append(None)
            copy = pltpu.make_async_remote_copy(
                src_ref=piece.at[s],
                dst_ref=piece_in.at[t % 4, h % 2],
                send_sem=send_sem.at[n],
                recv_sem=last_recv.at[t % 4, h % 2],
                device_id={"head": out_head, "tok": final_tok[s]},
                device_id_type=MESH,
            )
            if s:
                copy.start()
                sent[n] = copy
                continue
            local = pltpu.make_async_copy(piece.at[0], piece_in.at[t % 4, h % 2], last_recv.at[t % 4, h % 2])

            @pl.when(to_self)
            def _():
                local.start()

            @pl.when(jnp.logical_not(to_self))
            def _():
                copy.start()

            own_piece.append(copy)

    own_piece = []
    next(steps)
    for n in range(3):
        slot, count = GROUPS[n]
        next(steps)
        next(steps)
        whole(crossed, range(slot, slot + count))
        project(GROUPS[n])
        if n:
            finish(GROUPS[n - 1])
    next(steps)
    whole(crossed, (5, 6))
    project(GROUPS[3])
    finish(GROUPS[2])
    whole(crossed, (7,))
    project(GROUPS[4])
    finish(GROUPS[3])
    finish(GROUPS[4])
    for copy in sent:
        if copy is not None:
            copy.wait_send()

    @pl.when(jnp.logical_not(to_self))
    def _():
        own_piece[0].wait_send()

    store_rec.wait()
    for j in range(4):
        for half in range(2):
            pltpu.make_async_copy(piece_in.at[j, half], piece_in.at[j, half], last_recv.at[j, half]).wait()
            proj_v[16 * half:16 * half + 16, COLS * j:COLS * (j + 1)] = piece_in[j, half]
    store_proj = pltpu.make_async_copy(proj_v, proj_out, store_sem.at[1])
    store_proj.start()
    store_proj.wait()


def on_device(head_outputs, dec_bias, enc_bias, enc_weight, dec_weight, out_weight, active_ids):
    block = jax.ShapeDtypeStruct((BLOCK, WIDTH), BF16)
    vmem = pltpu.VMEM
    return pl.pallas_call(
        kernel,
        out_shape=(block, block),
        in_specs=[pl.BlockSpec(memory_space=pl.ANY)] * 7,
        out_specs=(pl.BlockSpec(memory_space=pl.ANY),) * 2,
        scratch_shapes=[
            vmem((BLOCK, WIDTH), BF16),
            vmem((1, WIDTH), F32),
            vmem((1, LATS), F32),
            vmem((WIDTH, LATS), BF16),
            vmem((LATS, WIDTH), BF16),
            vmem((WIDTH, COLS), BF16),
            vmem((TOKENS, 128), jnp.int32),
            vmem((TOKENS, WIDTH), BF16),
            vmem((HERE, TOKENS, 128), F32),
            vmem((TOKENS, 128), F32),
            vmem((HEADS, 8, TOKENS), F32),
            vmem((2 * PLANE, LATS), BF16),
            vmem((8, 64, WIDTH), F32),
            vmem((8, 64, WIDTH), BF16),
            vmem((8, 64, WIDTH), BF16),
            vmem((7, BLOCK, WIDTH), BF16),
            vmem((7, BLOCK, WIDTH), BF16),
            vmem((7, BLOCK, WIDTH), BF16),
            vmem((7, BLOCK, WIDTH), BF16),
            vmem((BLOCK, WIDTH), BF16),
            vmem((BLOCK, WIDTH), BF16),
            vmem((TOKENS, WIDTH), BF16),
            vmem((8, PLANE, COLS), BF16),
            vmem((HEADS, 8, 16, COLS), BF16),
            vmem((8, 16, COLS), BF16),
            vmem((4, 2, 16, COLS), BF16),
            vmem((BLOCK, WIDTH), BF16),
            pltpu.SemaphoreType.DMA((7,)),
            pltpu.SemaphoreType.DMA((MESSAGES,)),
            pltpu.SemaphoreType.DMA((MESSAGES,)),
            pltpu.SemaphoreType.DMA((4, 2)),
            pltpu.SemaphoreType.DMA((2,)),
        ],
        compiler_params=pltpu.CompilerParams(
            collective_id=0, has_side_effects=True, vmem_limit_bytes=60 * 2 ** 20
        ),
        cost_estimate=pl.CostEstimate(flops=9 * 10 ** 9, bytes_accessed=9 * 2 ** 20, transcendentals=0),
    )(
        head_outputs,
        dec_bias.reshape(1, WIDTH),
        enc_bias.reshape(1, LATS),
        enc_weight,
        dec_weight,
        out_weight,
        active_ids,
    )


def solution(mesh):
    return jax.shard_map(
        on_device,
        mesh=mesh,
        in_specs=(
            P("tok", "head"),
            P("head"),
            P("tok"),
            P("head", "tok"),
            P("tok", "head"),
            P("head", "tok"),
            P(),
        ),
        out_specs=(P("tok", "head"), P("tok", "head")),
        check_vma=False,
    )
```

time: 481 us -> 99.2 us (0.21)
  waiting for transfers between devices: 318 us -> 0 us
  Pallas kernels: 0 us -> 95.4 us
  blocking collectives: 75.7 us -> 0 us
  other arithmetic: 23.1 us -> 0 us
  matrix products: 22.5 us -> 0 us
  local copies, waits for them, and re-layouts: 24.9 us -> 2.95 us
  between operations: 13.8 us -> 0.64 us
    reduce_scatter x2 -> x0, waiting for transfers between devices: 163 us -> none  [the longest x1 125 us: on_device(): lax.psum_scatter(jnp.dot(latents.reshape(tokens, lat_count), dec_weight,...]
    all_gather x2 -> x0, waiting for transfers between devices: 155 us -> none  [the longest x1 80 us: on_device(): lax.all_gather(reconstruction, 'tok', axis=0, tiled=True)]
    pallas_call x0 -> x1, Pallas kernels: none -> 95.4 us  [on_device(): pl.pallas_call(kernel, out_shape=(block, block), in_specs=[pl.BlockSpec(m...]
    psum x1 -> x0, blocking collectives: 41.5 us -> none  [on_device(): value = jnp.maximum(lax.psum(picked, 'head') + bias, 0.0)]
    all_to_all x1 -> x0, blocking collectives: 34.2 us -> none  [on_device(): lax.all_to_all(partial_out, 'tok', split_axis=0, concat_axis=1, tiled=True)]
    dot_general x3 -> x0, matrix products: 22.5 us -> none  [the longest x1 10.5 us: on_device(): jnp.dot(lax.all_gather(centered, 'tok', axis=0, tiled=True), enc_weight,...]
    reduce_sum x1 -> x0, other arithmetic: 17.2 us -> none  [on_device(): jnp.sum(jnp.where(active, enc_bias.reshape(1, here, stride), 0.0), axis=2)]
    reshape x1 -> x0, local copies, waits for them, and re-layouts: 10.8 us -> none  [on_device(): partial_pre = jnp.dot(lax.all_gather(centered, 'tok', axis=0, tiled=True)...]
  transfers between devices with their start and end apart: 4 -> 0, of which waited for: 4 -> 0; matrix products, arithmetic and copies ran while one was open for 2% -> 0% of each run, Pallas kernels for 0% -> 0%
where the time goes in v2:
time: 99.2 us; the launch traced here: 99 us
  Pallas kernels  95.4 us (96%)
  local copies, waits for them, and re-layouts  2.95 us (3%)
    pallas_call x1, Pallas kernels, on_device(): pl.pallas_call(kernel, out_shape=(block, block), in_specs=[pl.BlockSpec(m...  95.4 us
    unnamed x2, local copies, waits for them, and re-layouts  2.95 us

profile of v2, /device:TPU:24, one launch (start us, length us, event | category | flops | bytes accessed | tf_op | source)
XLA Modules:
  0.0 99.0 jit_solution(13042324954763457911)
XLA Ops:
  0.6 95.4 %shard_map.86 = (bf16[32,1024]{1,0:T(8,128)(2,1)}, bf16[32,1024]{1,0:T(8,128)(2,1)}) custom-call(bf16[32,1024]{1,0:T(8,128)(2,1)} %ho.1, f32[1,1024]{1,0:T(1,128)} %bitcast.3, f32[1,2048]{1,0:T(1,128)} %bitcast.2, bf16[1024,2048]{1,0:T(8,128)(2,1)} %ew.1, bf16[2048,1024]{1,0:T(8,128)(2,1)} %dw.1, bf16[1024,256]{1,0:T(8,128)(2,1)} %ow.1, s32[1024,128]{1,0:T(8,128)} %ids.1), custom_call_target="tpu_custom_call" | custom-call | flops 8999999488 | bytes 9437184 | tf_op jit(solution)/shard_map/pallas_call | solution.py:414
  96.0 1.5 %copy.11 = bf16[32,1024]{1,0:T(8,128)(2,1)} copy(bf16[32,1024]{1,0:T(8,128)(2,1)} %get-tuple-element.4) | data formatting | bytes 131072
  97.5 1.5 %copy.12 = bf16[32,1024]{1,0:T(8,128)(2,1)} copy(bf16[32,1024]{1,0:T(8,128)(2,1)} %get-tuple-element.5) | data formatting | bytes 131072

commit v3 on v2

--- a/solution.py
+++ b/solution.py
@@ -14,8 +14,9 @@
 COLS = 256
 PLANE = 128
 PLANES = (0, -1, 1, -2, 2, -3, 3, 4)
+SLOT = {0: 0, -1: 1, 1: 2, -2: 3, 2: 4, -3: 5, 3: 6, -4: 7, 4: 7}
 GROUPS = ((0, 1), (1, 2), (3, 2), (5, 2), (7, 1))
-MESSAGES = 192
+MESSAGES = 224
 
 
 def row_of(slot, core, side):
@@ -27,7 +28,7 @@
     rec_out, proj_out,
     ho_v, db_v, eb_v, ew_v, dw_v, ow_v, ids_v,
     cen, off, vals, packed, lat, own_part, core_out, core_in,
-    zp_out, zp_in, zm_out, zm_in, x_out, x_in, rec,
+    zp_out, zp_in, zm_out, zm_in, x_out, x_in, rec, biases,
     part, part_in, piece, piece_in, proj_v,
     load_sem, send_sem, recv_sem, last_recv, store_sem,
 ):
@@ -39,7 +40,8 @@
         return ((side + dside) % 2) * 16 + ((z + dz) % 8) * 2 + (core + dcore) % 2
 
     zp, zm = {"tok": tok_of(0, 1, 0)}, {"tok": tok_of(0, 7, 0)}
-    xn, cn = {"tok": tok_of(1, 0, 0)}, {"tok": tok_of(0, 0, 1)}
+    zp_other, zm_other = {"tok": tok_of(1, 1, 0)}, {"tok": tok_of(1, 7, 0)}
+    xn, cn, far = {"tok": tok_of(1, 0, 0)}, {"tok": tok_of(0, 0, 1)}, {"tok": tok_of(0, 4, 0)}
     heads = [(h + k) % HEADS for k in range(HEADS)]
     out_head = t // 4
     my_part = h // 2
@@ -54,7 +56,7 @@
         loads[-1].start()
 
     barrier = pltpu.get_barrier_semaphore()
-    for target in (zp, zm, xn, cn):
+    for target in (zp, zm, zp_other, zm_other, xn, cn, far):
         pl.semaphore_signal(barrier, inc=1, device_id=target, device_id_type=MESH)
     for k in range(1, HEADS):
         pl.semaphore_signal(barrier, inc=1, device_id={"head": heads[k]}, device_id_type=MESH)
@@ -65,8 +67,37 @@
     loads[0].wait()
     loads[1].wait()
     cen[pl.ds(0, BLOCK), :] = (ho_v[...].astype(F32) - db_v[...]).astype(BF16)
-    vals[...] = jnp.zeros_like(vals)
-    pl.semaphore_wait(barrier, 4 + 7 + 8)
+
+    lane = lax.broadcasted_iota(jnp.int32, (PLANE, 128), 1)
+    lane_f = lane.astype(F32)
+
+    def offsets(slot):
+        def row(q):
+            return pl.multiple_of(
+                ((side + q % 2) % 2) * 512 + ((z + PLANES[slot] % 8) % 8) * 64 + ((core + q // 2) % 2) * BLOCK,
+                BLOCK,
+            )
+
+        rows = pl.ds(PLANE * slot, PLANE)
+        here = jnp.concatenate([ids_v[pl.ds(row(q), BLOCK), :] for q in range(4)], axis=0)
+        here = (here - t * LATS).astype(F32)
+        bias = jnp.zeros((PLANE, 128), F32)
+        for j in range(HERE):
+            column = jnp.sum(jnp.where(lane == t * HERE + j, here, 0.0), axis=1, keepdims=True) - j * STRIDE
+            column = jnp.broadcast_to(column, (PLANE, 128))
+            off[j, rows, :] = column
+            total = jnp.zeros((PLANE, 128), F32)
+            for q in range(4):
+                first = STRIDE * j + 128 * q
+                total += jnp.where(lane_f + 128.0 * q == column, eb_v[:, first:first + 128], 0.0)
+            bias += jnp.where(lane == j, jnp.sum(total, axis=1, keepdims=True), 0.0)
+        biases[rows, :] = bias
+
+    loads[2].wait()
+    loads[3].wait()
+    for slot in range(8):
+        offsets(slot)
+    pl.semaphore_wait(barrier, 7 + 7 + 8)
 
     sent = []
 
@@ -87,45 +118,46 @@
         def cross(slot, side):
             crossed[slot, side] = send(block(slot, 0, side), block(slot, 1, side), cn)
 
-        plus, minus = {}, {}
-
-        def go_plus(k, side):
-            if k == 3 and side == 1:
-                return
-            plus[k, side] = send(
-                block(2 * k - 1 if k else 0, 0, side), block(2 * k + 1, 0, side), zp
-            )
-
-        def go_minus(k, side):
-            if k == 3 and side == 0:
-                return
-            minus[k, side] = send(
-                block(2 * k, 0, side), block(2 * k + 2 if k < 3 else 7, 0, side), zm
-            )
-
+        moved = {}
+
+        def go(way, k, side, half):
+            slot = SLOT[way * k]
+            landing = SLOT[way * (k + 1)]
+            if k == 0:
+                src, side_there = part(0, 0, half), side
+                target = ((zp, zp_other), (zm, zm_other))[way > 0][side]
+            else:
+                if k == 3 and side != (way > 0):
+                    return
+                src, side_there = part(slot, side, half), side
+                target = (zp, zm)[way > 0]
+            moved[way, k, side, half] = send(src, part(landing, side_there, half), target)
+
+        def part(slot, side, half):
+            return buf.at[pl.ds(row_of(slot, 0, side) + 16 * half, 16), :]
+
+        for side in range(2):
+            for half in range(2):
+                for way in (-1, 1):
+                    go(way, 0, side, half)
         over = send(block(0, 0, 0), block(0, 0, 1), xn)
-        go_plus(0, 0)
-        go_minus(0, 0)
         cross(0, 0)
         yield
-        over.wait_recv()
-        go_plus(0, 1)
-        go_minus(0, 1)
-        cross(0, 1)
-        yield
-        for k in range(1, 4):
+        for k in range(1, 5):
             for side in range(2):
-                plus[k - 1, side].wait_recv()
-                go_plus(k, side)
-                cross(2 * k - 1, side)
-                minus[k - 1, side].wait_recv()
-                go_minus(k, side)
-                cross(2 * k, side)
-                yield
-        plus[3, 0].wait_recv()
-        cross(7, 0)
-        minus[3, 1].wait_recv()
-        cross(7, 1)
+                ways = [way for way in (-1, 1) if (way, k - 1, side, 0) in moved]
+                for half in range(2):
+                    for way in ways:
+                        moved[way, k - 1, side, half].wait_recv()
+                        if k < 4:
+                            go(way, k, side, half)
+                for way in ways:
+                    cross(SLOT[way * k], side)
+                if k == 1 and side == 1:
+                    over.wait_recv()
+                    cross(0, 1)
+                if k < 4:
+                    yield
         yield
 
     def whole(crossed, slots):
@@ -133,54 +165,26 @@
             for side in range(2):
                 crossed[slot, side].wait_recv()
 
-    lane = lax.broadcasted_iota(jnp.int32, (PLANE, 128), 1)
-    lane_f = lane.astype(F32)
-
     crossed = {}
     steps = gather(cen, crossed)
     next(steps)
-    loads[2].wait()
-
-    def offsets(slot):
-        row = lambda q: pl.multiple_of(
-            ((side + q % 2) % 2) * 512 + ((z + PLANES[slot] % 8) % 8) * 64 + ((core + q // 2) % 2) * BLOCK,
-            BLOCK,
-        )
-        here = jnp.concatenate([ids_v[pl.ds(row(q), BLOCK), :] for q in range(4)], axis=0)
-        here = (here - t * LATS).astype(F32)
-        for j in range(HERE):
-            column = jnp.sum(jnp.where(lane == t * HERE + j, here, 0.0), axis=1, keepdims=True)
-            off[j, pl.ds(PLANE * slot, PLANE), :] = jnp.broadcast_to(column - j * STRIDE, (PLANE, 128))
-
-    for slot in range(4):
-        offsets(slot)
-    next(steps)
-    for slot in range(4, 8):
-        offsets(slot)
-    loads[3].wait()
-    eb_v[...] = eb_v[...] * jnp.where(h == 0, 1.0, 0.0)
-
-    def encode(group, first, last):
+
+    def encode(group, latents):
         slot, count = group
         rows = pl.ds(PLANE * slot, PLANE * count)
-        lane_g = lax.broadcasted_iota(jnp.int32, (PLANE * count, 128), 1)
-        lane_gf = lane_g.astype(F32)
-
-        def body(j, carry):
-            lats = pl.ds(pl.multiple_of(j * STRIDE, STRIDE), STRIDE)
-            pre = jnp.dot(cen[rows, :], ew_v[:, lats], preferred_element_type=F32) + eb_v[:, lats]
+        lanes = lax.broadcasted_iota(jnp.int32, (PLANE * count, 128), 1)
+        lanes_f = lanes.astype(F32)
+        picked = jnp.zeros((PLANE * count, 128), F32) if latents[0] == 0 else vals[rows, :]
+        for j in latents:
+            pre = jnp.dot(
+                cen[rows, :], ew_v[:, STRIDE * j:STRIDE * (j + 1)], preferred_element_type=F32
+            )
             where = off[j, rows, :]
             total = jnp.zeros((PLANE * count, 128), F32)
             for q in range(4):
-                total += jnp.where(lane_gf + 128.0 * q == where, pre[:, 128 * q:128 * (q + 1)], 0.0)
-            picked = jnp.sum(total, axis=1, keepdims=True)
-            vals[rows, :] += jnp.where(lane_g == j, picked, 0.0)
-            return carry
-
-        lax.fori_loop(first, last, body, 0)
-
-    def pack(slot):
-        packed[0, :, pl.ds(PLANE * slot, PLANE)] = vals[pl.ds(PLANE * slot, PLANE), :].T[:8, :]
+                total += jnp.where(lanes_f + 128.0 * q == where, pre[:, 128 * q:128 * (q + 1)], 0.0)
+            picked += jnp.where(lanes == j, jnp.sum(total, axis=1, keepdims=True), 0.0)
+        vals[rows, :] = picked
 
     def pack(slots):
         for slot in slots:
@@ -197,17 +201,22 @@
     for n in range(3):
         slot, count = GROUPS[n]
         next(steps)
-        whole(crossed, range(slot, slot + count))
-        encode(GROUPS[n], 0, 2)
+        if n:
+            whole(crossed, range(slot, slot + count))
+            encode(GROUPS[n], (0, 1))
         next(steps)
-        encode(GROUPS[n], 2, 4)
+        if n:
+            encode(GROUPS[n], (2, 3))
+        else:
+            whole(crossed, (0,))
+            encode(GROUPS[0], (0, 1, 2, 3))
     next(steps)
     pack(range(0, 5))
     whole(crossed, (5, 6))
-    encode(GROUPS[3], 0, 4)
+    encode(GROUPS[3], (0, 1, 2, 3))
     pack((5, 6))
     whole(crossed, (7,))
-    encode(GROUPS[4], 0, 4)
+    encode(GROUPS[4], (0, 1, 2, 3))
     pack((7,))
 
     loads[5].wait()
@@ -221,9 +230,8 @@
             total = packed[0, :, rows]
             for k in range(1, HEADS):
                 total += packed[k, :, rows]
-            value = jnp.concatenate(
-                [jnp.maximum(total, 0.0), jnp.zeros((PLANE - 8, PLANE), F32)], axis=0
-            ).T
+            value = jnp.concatenate([total, jnp.zeros((PLANE - 8, PLANE), F32)], axis=0).T
+            value = jnp.maximum(value + biases[rows, :], 0.0)
             for j in range(HERE):
                 column = jnp.broadcast_to(value[:, j:j + 1], (PLANE, 128))
                 where = off[j, rows, :]
@@ -236,14 +244,14 @@
         lax.fori_loop(0, count, fill, 0)
 
         def body(n, carry):
-            cols = pl.ds(pl.multiple_of(n * 256, 256), 256)
+            cols = pl.ds(pl.multiple_of(n * 512, 512), 512)
             total = jnp.dot(lat[pl.ds(0, PLANE * count), :], dw_v[:, cols], preferred_element_type=F32)
             for i in range(count):
                 own_part[slot + i, :, cols] = total[PLANE * i:PLANE * i + 64]
                 core_out[slot + i, :, cols] = total[PLANE * i + 64:PLANE * (i + 1)].astype(BF16)
             return carry
 
-        lax.fori_loop(0, WIDTH // 256, body, 0)
+        lax.fori_loop(0, WIDTH // 512, body, 0, unroll=True)
         for i in range(count):
             crossed_sums[slot + i] = send(core_out.at[slot + i], core_in.at[slot + i], cn)
 
@@ -253,65 +261,60 @@
 
     plus, minus = {}, {}
 
-    def ring(out, arrived_at, table, target, n, slot, side, before):
+    def ring(out, arrived_at, table, target, n, slot, side):
         total = summed(slot, side)
-        if before is not None:
-            table[before].wait_recv()
-            total += arrived_at[before].astype(F32)
+        if n > 1:
+            table[n - 2].wait_recv()
+            total += arrived_at[n - 2].astype(F32)
         out[n] = total.astype(BF16)
         table[n] = send(out.at[n], arrived_at.at[n], target)
 
-    def go_plus(n, slot, side, before):
-        ring(zp_out, zp_in, plus, zp, n, slot, side, before)
-
-    def go_minus(n, slot, side, before):
-        ring(zm_out, zm_in, minus, zm, n, slot, side, before)
+    def ring_step(k):
+        for n, side in ((6 - 2 * k, 1), (7 - 2 * k, 0)):
+            diagonal = k == 1 and side == 1
+            ring(zp_out, zp_in, plus, zp_other if diagonal else zp, n, SLOT[k], side)
+            ring(zm_out, zm_in, minus, zm_other if diagonal else zm, n, SLOT[-k], side)
 
     def get(slot):
         for k in range(1, HEADS):
             arrived[slot, k].wait_recv()
 
+    def meet(*slots):
+        for slot in slots:
+            crossed_sums[slot].wait_recv()
+
+    get(5)
+    decode((5, 2))
     get(7)
     decode((7, 1))
-    get(5)
-    crossed_sums[7].wait_recv()
-    go_plus(0, 7, 1, None)
-    go_minus(0, 7, 0, None)
-    decode((5, 2))
+    meet(5, 6)
+    ring_step(3)
+    meet(7)
+    x_out[0] = summed(7, 1).astype(BF16)
+    x_far = send(x_out.at[0], x_in.at[0], xn)
     get(0)
-    crossed_sums[5].wait_recv()
-    crossed_sums[6].wait_recv()
-    go_plus(2, 6, 0, None)
-    go_minus(1, 5, 1, None)
-    go_plus(1, 6, 1, 0)
-    go_minus(2, 5, 0, 0)
     decode((3, 2))
-    crossed_sums[3].wait_recv()
-    crossed_sums[4].wait_recv()
-    go_minus(3, 3, 1, 1)
-    go_plus(4, 4, 0, 2)
-    go_plus(3, 4, 1, 1)
-    go_minus(4, 3, 0, 2)
     decode((1, 2))
-    crossed_sums[1].wait_recv()
-    crossed_sums[2].wait_recv()
-    go_minus(5, 1, 1, 3)
-    go_plus(5, 2, 1, 3)
-    go_plus(6, 2, 0, 4)
-    go_minus(6, 1, 0, 4)
     decode((0, 1))
-    crossed_sums[0].wait_recv()
-
-    def own(side, n):
+    meet(3, 4)
+    ring_step(2)
+    x_far.wait_recv()
+    x_out[1] = (summed(7, 0) + x_in[0].astype(F32)).astype(BF16)
+    x_far = send(x_out.at[1], x_in.at[1], far)
+    meet(0)
+    x_out[2] = summed(0, 1).astype(BF16)
+    x_near = send(x_out.at[2], x_in.at[2], xn)
+    meet(1, 2)
+    ring_step(1)
+    mine = summed(0, 0) + db_v[...]
+    x_near.wait_recv()
+    x_far.wait_recv()
+    mine += x_in[1].astype(F32) + x_in[2].astype(F32)
+    for n in (4, 5):
         plus[n].wait_recv()
         minus[n].wait_recv()
-        return summed(0, side) + (zp_in[n].astype(F32) + zm_in[n].astype(F32))
-
-    x_out[...] = own(1, 5).astype(BF16)
-    x_sum = send(x_out, x_in, xn)
-    mine = own(0, 6) + db_v[...]
-    x_sum.wait_recv()
-    rec[pl.ds(0, BLOCK), :] = (mine + x_in[...].astype(F32)).astype(BF16)
+        mine += zp_in[n].astype(F32) + zm_in[n].astype(F32)
+    rec[pl.ds(0, BLOCK), :] = mine.astype(BF16)
 
     crossed = {}
     steps = gather(rec, crossed)
@@ -373,7 +376,6 @@
             own_piece.append(copy)
 
     own_piece = []
-    next(steps)
     for n in range(3):
         slot, count = GROUPS[n]
         next(steps)
@@ -385,11 +387,10 @@
     next(steps)
     whole(crossed, (5, 6))
     project(GROUPS[3])
-    finish(GROUPS[2])
     whole(crossed, (7,))
     project(GROUPS[4])
-    finish(GROUPS[3])
-    finish(GROUPS[4])
+    for n in range(2, 5):
+        finish(GROUPS[n])
     for copy in sent:
         if copy is not None:
             copy.wait_send()
@@ -432,13 +433,14 @@
             vmem((8, 64, WIDTH), F32),
             vmem((8, 64, WIDTH), BF16),
             vmem((8, 64, WIDTH), BF16),
-            vmem((7, BLOCK, WIDTH), BF16),
-            vmem((7, BLOCK, WIDTH), BF16),
-            vmem((7, BLOCK, WIDTH), BF16),
-            vmem((7, BLOCK, WIDTH), BF16),
-            vmem((BLOCK, WIDTH), BF16),
-            vmem((BLOCK, WIDTH), BF16),
+            vmem((6, BLOCK, WIDTH), BF16),
+            vmem((6, BLOCK, WIDTH), BF16),
+            vmem((6, BLOCK, WIDTH), BF16),
+            vmem((6, BLOCK, WIDTH), BF16),
+            vmem((3, BLOCK, WIDTH), BF16),
+            vmem((3, BLOCK, WIDTH), BF16),
             vmem((TOKENS, WIDTH), BF16),
+            vmem((TOKENS, 128), F32),
             vmem((8, PLANE, COLS), BF16),
             vmem((HEADS, 8, 16, COLS), BF16),
             vmem((8, 16, COLS), BF16),

time: 99.2 us -> 91.9 us (0.926)
  Pallas kernels: 95.4 us -> 88.2 us
    pallas_call x1, Pallas kernels: 95.4 us -> 88.2 us  [on_device(): pl.pallas_call(kernel, out_shape=(block, block), in_specs=[pl.BlockSpec(m...]
where the time goes in v3:
time: 91.9 us; the launch traced here: 91.8 us
  Pallas kernels  88.2 us (96%)
  local copies, waits for them, and re-layouts  2.95 us (3%)
    pallas_call x1, Pallas kernels, on_device(): pl.pallas_call(kernel, out_shape=(block, block), in_specs=[pl.BlockSpec(m...  88.2 us
    unnamed x2, local copies, waits for them, and re-layouts  2.95 us

profile of v3, /device:TPU:24, one launch (start us, length us, event | category | flops | bytes accessed | tf_op | source)
XLA Modules:
  0.0 91.8 jit_solution(834665968447654721)
XLA Ops:
  0.6 88.2 %shard_map.86 = (bf16[32,1024]{1,0:T(8,128)(2,1)}, bf16[32,1024]{1,0:T(8,128)(2,1)}) custom-call(bf16[32,1024]{1,0:T(8,128)(2,1)} %ho.1, f32[1,1024]{1,0:T(1,128)} %bitcast.3, f32[1,2048]{1,0:T(1,128)} %bitcast.2, bf16[1024,2048]{1,0:T(8,128)(2,1)} %ew.1, bf16[2048,1024]{1,0:T(8,128)(2,1)} %dw.1, bf16[1024,256]{1,0:T(8,128)(2,1)} %ow.1, s32[1024,128]{1,0:T(8,128)} %ids.1), custom_call_target="tpu_custom_call" | custom-call | flops 8999999488 | bytes 9437184 | tf_op jit(solution)/shard_map/pallas_call | solution.py:415
  88.8 1.5 %copy.11 = bf16[32,1024]{1,0:T(8,128)(2,1)} copy(bf16[32,1024]{1,0:T(8,128)(2,1)} %get-tuple-element.4) | data formatting | bytes 131072
  90.3 1.5 %copy.12 = bf16[32,1024]{1,0:T(8,128)(2,1)} copy(bf16[32,1024]{1,0:T(8,128)(2,1)} %get-tuple-element.5) | data formatting | bytes 131072

commit v4 on v3

--- a/solution.py
+++ b/solution.py
@@ -16,7 +16,7 @@
 PLANES = (0, -1, 1, -2, 2, -3, 3, 4)
 SLOT = {0: 0, -1: 1, 1: 2, -2: 3, 2: 4, -3: 5, 3: 6, -4: 7, 4: 7}
 GROUPS = ((0, 1), (1, 2), (3, 2), (5, 2), (7, 1))
-MESSAGES = 224
+MESSAGES = 256
 
 
 def row_of(slot, core, side):
@@ -121,17 +121,13 @@
         moved = {}
 
         def go(way, k, side, half):
-            slot = SLOT[way * k]
-            landing = SLOT[way * (k + 1)]
             if k == 0:
-                src, side_there = part(0, 0, half), side
+                src = part(0, 0, half)
                 target = ((zp, zp_other), (zm, zm_other))[way > 0][side]
             else:
-                if k == 3 and side != (way > 0):
-                    return
-                src, side_there = part(slot, side, half), side
+                src = part(SLOT[way * k], side, half)
                 target = (zp, zm)[way > 0]
-            moved[way, k, side, half] = send(src, part(landing, side_there, half), target)
+            moved[way, k, side, half] = send(src, part(SLOT[way * (k + 1)], side, half), target)
 
         def part(slot, side, half):
             return buf.at[pl.ds(row_of(slot, 0, side) + 16 * half, 16), :]
@@ -140,25 +136,29 @@
             for half in range(2):
                 for way in (-1, 1):
                     go(way, 0, side, half)
+        direct = send(block(0, 0, 0), block(7, 0, 0), far)
         over = send(block(0, 0, 0), block(0, 0, 1), xn)
         cross(0, 0)
         yield
-        for k in range(1, 5):
+        for k in range(1, 4):
             for side in range(2):
-                ways = [way for way in (-1, 1) if (way, k - 1, side, 0) in moved]
                 for half in range(2):
-                    for way in ways:
+                    for way in (-1, 1):
                         moved[way, k - 1, side, half].wait_recv()
-                        if k < 4:
+                        if k < 3:
                             go(way, k, side, half)
-                for way in ways:
+                for way in (-1, 1):
                     cross(SLOT[way * k], side)
                 if k == 1 and side == 1:
                     over.wait_recv()
                     cross(0, 1)
-                if k < 4:
-                    yield
-        yield
+                    direct.wait_recv()
+                    direct = send(block(7, 0, 0), block(7, 0, 1), xn)
+                    cross(7, 0)
+                if k == 3 and side == 0:
+                    direct.wait_recv()
+                    cross(7, 1)
+                yield
 
     def whole(crossed, slots):
         for slot in slots:
@@ -198,26 +198,24 @@
 
     arrived = {}
     loads[4].wait()
-    for n in range(3):
+    next(steps)
+    next(steps)
+    whole(crossed, (0,))
+    encode(GROUPS[0], (0, 1, 2, 3))
+    for n in (1, 2):
         slot, count = GROUPS[n]
         next(steps)
-        if n:
-            whole(crossed, range(slot, slot + count))
-            encode(GROUPS[n], (0, 1))
+        whole(crossed, range(slot, slot + count))
+        encode(GROUPS[n], (0, 1))
         next(steps)
-        if n:
-            encode(GROUPS[n], (2, 3))
-        else:
-            whole(crossed, (0,))
-            encode(GROUPS[0], (0, 1, 2, 3))
-    next(steps)
+        encode(GROUPS[n], (2, 3))
     pack(range(0, 5))
+    whole(crossed, (7,))
+    encode(GROUPS[4], (0, 1, 2, 3))
+    pack((7,))
     whole(crossed, (5, 6))
     encode(GROUPS[3], (0, 1, 2, 3))
     pack((5, 6))
-    whole(crossed, (7,))
-    encode(GROUPS[4], (0, 1, 2, 3))
-    pack((7,))
 
     loads[5].wait()
     crossed_sums = {}
@@ -243,15 +241,10 @@
 
         lax.fori_loop(0, count, fill, 0)
 
-        def body(n, carry):
-            cols = pl.ds(pl.multiple_of(n * 512, 512), 512)
-            total = jnp.dot(lat[pl.ds(0, PLANE * count), :], dw_v[:, cols], preferred_element_type=F32)
-            for i in range(count):
-                own_part[slot + i, :, cols] = total[PLANE * i:PLANE * i + 64]
-                core_out[slot + i, :, cols] = total[PLANE * i + 64:PLANE * (i + 1)].astype(BF16)
-            return carry
-
-        lax.fori_loop(0, WIDTH // 512, body, 0, unroll=True)
+        total = jnp.dot(lat[pl.ds(0, PLANE * count), :], dw_v[...], preferred_element_type=F32)
+        for i in range(count):
+            own_part[slot + i] = total[PLANE * i:PLANE * i + 64]
+            core_out[slot + i] = total[PLANE * i + 64:PLANE * (i + 1)].astype(BF16)
         for i in range(count):
             crossed_sums[slot + i] = send(core_out.at[slot + i], core_in.at[slot + i], cn)
 
@@ -261,19 +254,21 @@
 
     plus, minus = {}, {}
 
-    def ring(out, arrived_at, table, target, n, slot, side):
-        total = summed(slot, side)
-        if n > 1:
-            table[n - 2].wait_recv()
-            total += arrived_at[n - 2].astype(F32)
+    def ring(out, arrived_at, table, target, n, slot, piece):
+        rows = pl.ds(16 * piece, 16)
+        total = own_part[slot, rows, :] + core_in[slot, rows, :].astype(F32)
+        if n > 3:
+            table[n - 4].wait_recv()
+            total += arrived_at[n - 4].astype(F32)
         out[n] = total.astype(BF16)
         table[n] = send(out.at[n], arrived_at.at[n], target)
 
     def ring_step(k):
-        for n, side in ((6 - 2 * k, 1), (7 - 2 * k, 0)):
-            diagonal = k == 1 and side == 1
-            ring(zp_out, zp_in, plus, zp_other if diagonal else zp, n, SLOT[k], side)
-            ring(zm_out, zm_in, minus, zm_other if diagonal else zm, n, SLOT[-k], side)
+        for i, piece in enumerate((2, 3, 0, 1)):
+            diagonal = k == 1 and piece > 1
+            n = 4 * (3 - k) + i
+            ring(zp_out, zp_in, plus, zp_other if diagonal else zp, n, SLOT[k], piece)
+            ring(zm_out, zm_in, minus, zm_other if diagonal else zm, n, SLOT[-k], piece)
 
     def get(slot):
         for k in range(1, HEADS):
@@ -283,38 +278,41 @@
         for slot in slots:
             crossed_sums[slot].wait_recv()
 
-    get(5)
-    decode((5, 2))
     get(7)
     decode((7, 1))
-    meet(5, 6)
-    ring_step(3)
+    get(0)
+    decode((3, 2))
     meet(7)
     x_out[0] = summed(7, 1).astype(BF16)
     x_far = send(x_out.at[0], x_in.at[0], xn)
-    get(0)
-    decode((3, 2))
+    get(5)
+    decode((5, 2))
+    decode((0, 1))
+    meet(5, 6)
+    ring_step(3)
     decode((1, 2))
-    decode((0, 1))
-    meet(3, 4)
-    ring_step(2)
     x_far.wait_recv()
     x_out[1] = (summed(7, 0) + x_in[0].astype(F32)).astype(BF16)
     x_far = send(x_out.at[1], x_in.at[1], far)
     meet(0)
     x_out[2] = summed(0, 1).astype(BF16)
     x_near = send(x_out.at[2], x_in.at[2], xn)
+    meet(3, 4)
+    ring_step(2)
     meet(1, 2)
     ring_step(1)
     mine = summed(0, 0) + db_v[...]
     x_near.wait_recv()
     x_far.wait_recv()
     mine += x_in[1].astype(F32) + x_in[2].astype(F32)
-    for n in (4, 5):
-        plus[n].wait_recv()
-        minus[n].wait_recv()
-        mine += zp_in[n].astype(F32) + zm_in[n].astype(F32)
-    rec[pl.ds(0, BLOCK), :] = mine.astype(BF16)
+    for half in range(2):
+        rows = slice(16 * half, 16 * half + 16)
+        total = mine[rows]
+        for n in (8 + half, 10 + half):
+            plus[n].wait_recv()
+            minus[n].wait_recv()
+            total += zp_in[n].astype(F32) + zm_in[n].astype(F32)
+        rec[rows, :] = total.astype(BF16)
 
     crossed = {}
     steps = gather(rec, crossed)
@@ -376,21 +374,27 @@
             own_piece.append(copy)
 
     own_piece = []
-    for n in range(3):
-        slot, count = GROUPS[n]
-        next(steps)
-        next(steps)
-        whole(crossed, range(slot, slot + count))
-        project(GROUPS[n])
-        if n:
-            finish(GROUPS[n - 1])
-    next(steps)
+    next(steps)
+    next(steps)
+    whole(crossed, (0,))
+    project(GROUPS[0])
+    next(steps)
+    whole(crossed, (1, 2))
+    project(GROUPS[1])
+    next(steps)
+    finish(GROUPS[0])
+    next(steps)
+    whole(crossed, (3, 4))
+    project(GROUPS[2])
+    next(steps)
+    finish(GROUPS[1])
+    whole(crossed, (7,))
+    project(GROUPS[4])
     whole(crossed, (5, 6))
     project(GROUPS[3])
-    whole(crossed, (7,))
-    project(GROUPS[4])
-    for n in range(2, 5):
-        finish(GROUPS[n])
+    finish(GROUPS[2])
+    finish(GROUPS[4])
+    finish(GROUPS[3])
     for copy in sent:
         if copy is not None:
             copy.wait_send()
@@ -409,10 +413,21 @@
     store_proj.wait()
 
 
+def hand_over(rec_in, proj_in, rec_out, proj_out, sem):
+    copies = [
+        pltpu.make_async_copy(rec_in, rec_out, sem.at[0]),
+        pltpu.make_async_copy(proj_in, proj_out, sem.at[1]),
+    ]
+    for copy in copies:
+        copy.start()
+    for copy in copies:
+        copy.wait()
+
+
 def on_device(head_outputs, dec_bias, enc_bias, enc_weight, dec_weight, out_weight, active_ids):
     block = jax.ShapeDtypeStruct((BLOCK, WIDTH), BF16)
     vmem = pltpu.VMEM
-    return pl.pallas_call(
+    results = pl.pallas_call(
         kernel,
         out_shape=(block, block),
         in_specs=[pl.BlockSpec(memory_space=pl.ANY)] * 7,
@@ -433,10 +448,10 @@
             vmem((8, 64, WIDTH), F32),
             vmem((8, 64, WIDTH), BF16),
             vmem((8, 64, WIDTH), BF16),
-            vmem((6, BLOCK, WIDTH), BF16),
-            vmem((6, BLOCK, WIDTH), BF16),
-            vmem((6, BLOCK, WIDTH), BF16),
-            vmem((6, BLOCK, WIDTH), BF16),
+            vmem((12, 16, WIDTH), BF16),
+            vmem((12, 16, WIDTH), BF16),
+            vmem((12, 16, WIDTH), BF16),
+            vmem((12, 16, WIDTH), BF16),
             vmem((3, BLOCK, WIDTH), BF16),
             vmem((3, BLOCK, WIDTH), BF16),
             vmem((TOKENS, WIDTH), BF16),
@@ -465,6 +480,13 @@
         out_weight,
         active_ids,
     )
+    return pl.pallas_call(
+        hand_over,
+        out_shape=(block, block),
+        in_specs=[pl.BlockSpec(memory_space=pl.ANY)] * 2,
+        out_specs=(pl.BlockSpec(memory_space=pl.ANY),) * 2,
+        scratch_shapes=[pltpu.SemaphoreType.DMA((2,))],
+    )(*results)
 
 
 def solution(mesh):

time: 91.9 us -> 93 us (1.012)
  Pallas kernels: 88.2 us -> 92.1 us
  local copies, waits for them, and re-layouts: 2.95 us -> 0 us
    pallas_call x0 -> x1, Pallas kernels: none -> 5.09 us  [on_device(): pl.pallas_call(hand_over, out_shape=(block, block), in_specs=[pl.BlockSpe...]
    unnamed x2 -> x0, local copies, waits for them, and re-layouts: 2.95 us -> none
    pallas_call x1, Pallas kernels: 88.2 us -> 87 us  [on_device(): pl.pallas_call(kernel, out_shape=(block, block), in_specs=[pl.BlockSpec(m...]
where the time goes in v4:
time: 93 us; the launch traced here: 92.9 us
  Pallas kernels  92.1 us (99%)
    pallas_call x1, Pallas kernels, on_device(): pl.pallas_call(kernel, out_shape=(block, block), in_specs=[pl.BlockSpec(m...  87 us
    pallas_call x1, Pallas kernels, on_device(): pl.pallas_call(hand_over, out_shape=(block, block), in_specs=[pl.BlockSpe...  5.09 us

profile of v4, /device:TPU:24, one launch (start us, length us, event | category | flops | bytes accessed | tf_op | source)
XLA Modules:
  0.0 92.9 jit_solution(4586754379914805047)
XLA Ops:
  0.6 87.0 %shard_map.86 = (bf16[32,1024]{1,0:T(8,128)(2,1)}, bf16[32,1024]{1,0:T(8,128)(2,1)}) custom-call(bf16[32,1024]{1,0:T(8,128)(2,1)} %ho.1, f32[1,1024]{1,0:T(1,128)} %bitcast.3, f32[1,2048]{1,0:T(1,128)} %bitcast.2, bf16[1024,2048]{1,0:T(8,128)(2,1)} %ew.1, bf16[2048,1024]{1,0:T(8,128)(2,1)} %dw.1, bf16[1024,256]{1,0:T(8,128)(2,1)} %ow.1, s32[1024,128]{1,0:T(8,128)} %ids.1), custom_call_target="tpu_custom_call" | custom-call | flops 8999999488 | bytes 9437184 | tf_op jit(solution)/shard_map/pallas_call | solution.py:430
  87.7 5.1 %shard_map.87 = (bf16[32,1024]{1,0:T(8,128)(2,1)}, bf16[32,1024]{1,0:T(8,128)(2,1)}) custom-call(bf16[32,1024]{1,0:T(8,128)(2,1)} %get-tuple-element.4.rec_in, bf16[32,1024]{1,0:T(8,128)(2,1)} %get-tuple-element.5.proj_in), custom_call_target="tpu_custom_call" | custom-call | tf_op jit(solution)/shard_map/pallas_call | solution.py:483

commit v5 on v4

--- a/solution.py
+++ b/solution.py
@@ -25,7 +25,7 @@
 
 def kernel(
     ho, dbias, ebias, ew, dw, ow, ids,
-    rec_out, proj_out,
+    both_out,
     ho_v, db_v, eb_v, ew_v, dw_v, ow_v, ids_v,
     cen, off, vals, packed, lat, own_part, core_out, core_in,
     zp_out, zp_in, zm_out, zm_in, x_out, x_in, rec, biases,
@@ -209,13 +209,15 @@
         encode(GROUPS[n], (0, 1))
         next(steps)
         encode(GROUPS[n], (2, 3))
-    pack(range(0, 5))
+        if n == 1:
+            pack((0, 1, 2))
+    whole(crossed, (5, 6))
+    encode(GROUPS[3], (0, 1, 2, 3))
+    pack((5, 6))
     whole(crossed, (7,))
     encode(GROUPS[4], (0, 1, 2, 3))
     pack((7,))
-    whole(crossed, (5, 6))
-    encode(GROUPS[3], (0, 1, 2, 3))
-    pack((5, 6))
+    pack((3, 4))
 
     loads[5].wait()
     crossed_sums = {}
@@ -278,25 +280,26 @@
         for slot in slots:
             crossed_sums[slot].wait_recv()
 
+    get(0)
+    decode((0, 1))
+    get(5)
+    decode((5, 2))
     get(7)
     decode((7, 1))
-    get(0)
-    decode((3, 2))
+    meet(5, 6)
+    ring_step(3)
     meet(7)
     x_out[0] = summed(7, 1).astype(BF16)
     x_far = send(x_out.at[0], x_in.at[0], xn)
-    get(5)
-    decode((5, 2))
-    decode((0, 1))
-    meet(5, 6)
-    ring_step(3)
+    meet(0)
+    x_out[2] = summed(0, 1).astype(BF16)
+    x_near = send(x_out.at[2], x_in.at[2], xn)
+    get(3)
+    decode((3, 2))
     decode((1, 2))
     x_far.wait_recv()
     x_out[1] = (summed(7, 0) + x_in[0].astype(F32)).astype(BF16)
     x_far = send(x_out.at[1], x_in.at[1], far)
-    meet(0)
-    x_out[2] = summed(0, 1).astype(BF16)
-    x_near = send(x_out.at[2], x_in.at[2], xn)
     meet(3, 4)
     ring_step(2)
     meet(1, 2)
@@ -317,7 +320,7 @@
     crossed = {}
     steps = gather(rec, crossed)
     next(steps)
-    store_rec = pltpu.make_async_copy(rec.at[pl.ds(0, BLOCK), :], rec_out, store_sem.at[0])
+    store_rec = pltpu.make_async_copy(rec.at[pl.ds(0, BLOCK), :], both_out.at[0], store_sem.at[0])
     store_rec.start()
     loads[6].wait()
     spread = {}
@@ -387,11 +390,11 @@
     whole(crossed, (3, 4))
     project(GROUPS[2])
     next(steps)
-    finish(GROUPS[1])
     whole(crossed, (7,))
     project(GROUPS[4])
     whole(crossed, (5, 6))
     project(GROUPS[3])
+    finish(GROUPS[1])
     finish(GROUPS[2])
     finish(GROUPS[4])
     finish(GROUPS[3])
@@ -408,20 +411,9 @@
         for half in range(2):
             pltpu.make_async_copy(piece_in.at[j, half], piece_in.at[j, half], last_recv.at[j, half]).wait()
             proj_v[16 * half:16 * half + 16, COLS * j:COLS * (j + 1)] = piece_in[j, half]
-    store_proj = pltpu.make_async_copy(proj_v, proj_out, store_sem.at[1])
+    store_proj = pltpu.make_async_copy(proj_v, both_out.at[1], store_sem.at[1])
     store_proj.start()
     store_proj.wait()
-
-
-def hand_over(rec_in, proj_in, rec_out, proj_out, sem):
-    copies = [
-        pltpu.make_async_copy(rec_in, rec_out, sem.at[0]),
-        pltpu.make_async_copy(proj_in, proj_out, sem.at[1]),
-    ]
-    for copy in copies:
-        copy.start()
-    for copy in copies:
-        copy.wait()
 
 
 def on_device(head_outputs, dec_bias, enc_bias, enc_weight, dec_weight, out_weight, active_ids):
@@ -429,9 +421,9 @@
     vmem = pltpu.VMEM
     results = pl.pallas_call(
         kernel,
-        out_shape=(block, block),
+        out_shape=jax.ShapeDtypeStruct((2, BLOCK, WIDTH), BF16),
         in_specs=[pl.BlockSpec(memory_space=pl.ANY)] * 7,
-        out_specs=(pl.BlockSpec(memory_space=pl.ANY),) * 2,
+        out_specs=pl.BlockSpec(memory_space=pl.ANY),
         scratch_shapes=[
             vmem((BLOCK, WIDTH), BF16),
             vmem((1, WIDTH), F32),
@@ -480,13 +472,7 @@
         out_weight,
         active_ids,
     )
-    return pl.pallas_call(
-        hand_over,
-        out_shape=(block, block),
-        in_specs=[pl.BlockSpec(memory_space=pl.ANY)] * 2,
-        out_specs=(pl.BlockSpec(memory_space=pl.ANY),) * 2,
-        scratch_shapes=[pltpu.SemaphoreType.DMA((2,))],
-    )(*results)
+    return results[0], results[1]
 
 
 def solution(mesh):

time: 93 us -> 88.7 us (0.954)
  Pallas kernels: 92.1 us -> 86.3 us
  local copies, waits for them, and re-layouts: 0 us -> 1.53 us
    pallas_call x2 -> x1, Pallas kernels: 92.1 us -> 86.3 us  [on_device(): pl.pallas_call(kernel, out_shape=jax.ShapeDtypeStruct((2, BLOCK, WIDTH),...]
    squeeze x0 -> x1, local copies, waits for them, and re-layouts: none -> 1.53 us  [on_device(): return (results[0], results[1])]
where the time goes in v5:
time: 88.7 us; the launch traced here: 88.5 us
  Pallas kernels  86.3 us (97%)
  local copies, waits for them, and re-layouts  1.53 us (2%)
    pallas_call x1, Pallas kernels, on_device(): pl.pallas_call(kernel, out_shape=jax.ShapeDtypeStruct((2, BLOCK, WIDTH),...  86.3 us

profile of v5, /device:TPU:24, one launch (start us, length us, event | category | flops | bytes accessed | tf_op | source)
XLA Modules:
  0.0 88.5 jit_solution(17395920460939279643)
XLA Ops:
  0.6 86.3 %shard_map.86 = bf16[2,32,1024]{2,1,0:T(8,128)(2,1)} custom-call(bf16[32,1024]{1,0:T(8,128)(2,1)} %ho.1, f32[1,1024]{1,0:T(1,128)} %bitcast.7, f32[1,2048]{1,0:T(1,128)} %bitcast.6, bf16[1024,2048]{1,0:T(8,128)(2,1)} %ew.1, bf16[2048,1024]{1,0:T(8,128)(2,1)} %dw.1, bf16[1024,256]{1,0:T(8,128)(2,1)} %ow.1, s32[1024,128]{1,0:T(8,128)} %ids.1), custom_call_target="tpu_custom_call" | custom-call | flops 8999999488 | bytes 9437184 | tf_op jit(solution)/shard_map/pallas_call | solution.py:422
  87.0 1.5 %slice_bitcast_fusion = (bf16[32,1024]{1,0:T(8,128)(2,1)}, bf16[32,1024]{1,0:T(8,128)(2,1)}) fusion(bf16[2,32,1024]{2,1,0:T(8,128)(2,1)} %shard_map.86), kind=kLoop, calls=%fused_computation | loop fusion | bytes 262144 | tf_op jit(solution)/shard_map/squeeze | solution.py:475

commit v6 on v5

--- a/solution.py
+++ b/solution.py
@@ -296,12 +296,12 @@
     x_near = send(x_out.at[2], x_in.at[2], xn)
     get(3)
     decode((3, 2))
-    decode((1, 2))
     x_far.wait_recv()
     x_out[1] = (summed(7, 0) + x_in[0].astype(F32)).astype(BF16)
     x_far = send(x_out.at[1], x_in.at[1], far)
     meet(3, 4)
     ring_step(2)
+    decode((1, 2))
     meet(1, 2)
     ring_step(1)
     mine = summed(0, 0) + db_v[...]
@@ -318,11 +318,14 @@
         rec[rows, :] = total.astype(BF16)
 
     crossed = {}
+    before = len(sent)
     steps = gather(rec, crossed)
     next(steps)
     store_rec = pltpu.make_async_copy(rec.at[pl.ds(0, BLOCK), :], both_out.at[0], store_sem.at[0])
     store_rec.start()
     loads[6].wait()
+    for copy in sent[:before]:
+        copy.wait_send()
     spread = {}
 
     def project(group):
@@ -398,21 +401,21 @@
     finish(GROUPS[2])
     finish(GROUPS[4])
     finish(GROUPS[3])
-    for copy in sent:
-        if copy is not None:
-            copy.wait_send()
-
-    @pl.when(jnp.logical_not(to_self))
-    def _():
-        own_piece[0].wait_send()
-
-    store_rec.wait()
     for j in range(4):
         for half in range(2):
             pltpu.make_async_copy(piece_in.at[j, half], piece_in.at[j, half], last_recv.at[j, half]).wait()
             proj_v[16 * half:16 * half + 16, COLS * j:COLS * (j + 1)] = piece_in[j, half]
     store_proj = pltpu.make_async_copy(proj_v, both_out.at[1], store_sem.at[1])
     store_proj.start()
+    for copy in sent[before:]:
+        if copy is not None:
+            copy.wait_send()
+
+    @pl.when(jnp.logical_not(to_self))
+    def _():
+        own_piece[0].wait_send()
+
+    store_rec.wait()
     store_proj.wait()
 
 

time: 88.7 us -> 88.3 us (level)
  no operation moved by 1% of the time
where the time goes in v6:
time: 88.3 us; the launch traced here: 88.1 us
  Pallas kernels  85.9 us (97%)
  local copies, waits for them, and re-layouts  1.53 us (2%)
    pallas_call x1, Pallas kernels, on_device(): pl.pallas_call(kernel, out_shape=jax.ShapeDtypeStruct((2, BLOCK, WIDTH),...  85.9 us

profile of v6, /device:TPU:24, one launch (start us, length us, event | category | flops | bytes accessed | tf_op | source)
XLA Modules:
  0.0 88.1 jit_solution(12065925255546323516)
XLA Ops:
  0.6 85.9 %shard_map.86 = bf16[2,32,1024]{2,1,0:T(8,128)(2,1)} custom-call(bf16[32,1024]{1,0:T(8,128)(2,1)} %ho.1, f32[1,1024]{1,0:T(1,128)} %bitcast.7, f32[1,2048]{1,0:T(1,128)} %bitcast.6, bf16[1024,2048]{1,0:T(8,128)(2,1)} %ew.1, bf16[2048,1024]{1,0:T(8,128)(2,1)} %dw.1, bf16[1024,256]{1,0:T(8,128)(2,1)} %ow.1, s32[1024,128]{1,0:T(8,128)} %ids.1), custom_call_target="tpu_custom_call" | custom-call | flops 8999999488 | bytes 9437184 | tf_op jit(solution)/shard_map/pallas_call | solution.py:425
  86.6 1.5 %slice_bitcast_fusion = (bf16[32,1024]{1,0:T(8,128)(2,1)}, bf16[32,1024]{1,0:T(8,128)(2,1)}) fusion(bf16[2,32,1024]{2,1,0:T(8,128)(2,1)} %shard_map.86), kind=kLoop, calls=%fused_computation | loop fusion | bytes 262144 | tf_op jit(solution)/shard_map/squeeze | solution.py:478
